TPU v7x, 128 devices: a whole 4x4x4 slice. The times are simulated.
128 devices in a mesh: seq: 16 (over y, x), head: 8 (over z, core).
Axes of the slice: x: 4, y: 4, z: 4, core: 2. Of those that a mesh axis runs over, the one named last changes fastest.
Arguments:
- queries: bfloat16 [32768, 2048], P(('seq', 'head')), may hold values from -8 to 8
- keys: bfloat16 [32768, 2048], P(('seq', 'head')), may hold values from -8 to 8
- values: bfloat16 [32768, 2048], P(('seq', 'head')), may hold values from -6 to 6
- lengths: int32 [16, 3], replicated, may hold values from 1 to 10, 16 in all within a row
- plan: int32 [256], replicated, may hold values from 0 to 255, as said below
Outputs:
- attended: bfloat16 [32768, 2048], P(('seq', 'head'))
Inputs may be any that keep to these rules, and one draw needn't show every extreme that they name: `lengths`: each row sums to 16. A permutation of the block indices. Stream block b lies in group b // 16 and goes to group plan[b] // 16; each group sends exactly 2 blocks to each of 8 distinct groups, among them itself, the next group (index + 1, counted round) and the group 16 // 2 away (index + 8, counted round), and none to any other, and the 2 blocks of one device go to distinct groups.
All inputs are finite; a program needn't handle non-finite values.
Results may differ from a plain program's by a relative error of at most 0.0047.
Values may be sent and summed in bfloat16 or wider, within the bound.
A program may use at most 128 MiB of HBM per device.

v0:
```python
import math

import jax
import jax.numpy as jnp
from jax import lax
from jax.sharding import PartitionSpec as P

HEAD_DIM = 128
BLOCK = 128


def attend(q_rows, k_rows, v_rows, lens):
    total = q_rows.shape[0]
    width = q_rows.shape[1]
    heads_here = width // HEAD_DIM
    q_three = q_rows.reshape(total, heads_here, HEAD_DIM)
    k_three = k_rows.reshape(total, heads_here, HEAD_DIM)
    v_three = v_rows.reshape(total, heads_here, HEAD_DIM)
    ends = jnp.cumsum(lens) * BLOCK
    positions = jnp.arange(total, dtype=jnp.int32)
    record = jnp.sum((positions[:, None] >= ends[None, :]).astype(jnp.int32), axis=1)
    factor = 1.0 / math.sqrt(HEAD_DIM)
    span = min(512, total)
    pieces = []
    for start in range(0, total, span):
        stop = start + span
        scores = (
            jnp.einsum(
                "qhd,khd->hqk",
                q_three[start:stop],
                k_three[:stop],
                preferred_element_type=jnp.float32,
            )
            * factor
        )
        visible = (record[start:stop, None] == record[None, :stop]) & (
            positions[None, :stop] <= positions[start:stop, None]
        )
        scores = jnp.where(visible[None], scores, -1e30)
        peak = jnp.max(scores, axis=-1, keepdims=True)
        expo = jnp.exp(scores - peak)
        weights = (expo / jnp.sum(expo, axis=-1, keepdims=True)).astype(jnp.bfloat16)
        output = jnp.einsum(
            "hqk,khd->qhd", weights, v_three[:stop], preferred_element_type=jnp.float32
        )
        pieces.append(output.astype(jnp.bfloat16).reshape(span, width))
    return jnp.concatenate(pieces, axis=0)


def owner_of(place_flat, arrived_flat, count):
    slots = jnp.arange(count, dtype=jnp.int32)[:, None]
    sources = jnp.arange(place_flat.shape[0], dtype=jnp.int32)[None, :]
    match = (place_flat[None, :] == slots) & arrived_flat[None, :]
    return jnp.sum(jnp.where(match, sources, 0), axis=1)


def local(queries, keys, values, lengths, plan):
    rows_dev = queries.shape[0]
    width = queries.shape[1]
    seq_count = lax.axis_size("seq")
    head_count = lax.axis_size("head")
    per_dev = rows_dev // BLOCK
    group_blocks = per_dev * head_count
    group_rows = group_blocks * BLOCK
    slice_width = width // head_count
    group_idx = lax.axis_index("seq")
    member_idx = lax.axis_index("head")
    my_lens = lax.dynamic_index_in_dim(lengths, group_idx, 0, keepdims=False)
    dev_count = seq_count * head_count
    dev_table = plan.reshape(dev_count, per_dev)
    dev_dest = dev_table // group_blocks
    dev_slot = dev_table % group_blocks
    me_flat = group_idx * head_count + member_idx
    mine = lax.dynamic_index_in_dim(dev_dest, me_flat, 0, keepdims=False)
    local_ids = jnp.arange(per_dev, dtype=jnp.int32)
    targets = jnp.arange(seq_count, dtype=jnp.int32)[:, None]
    hit_out = mine[None, :] == targets
    pick = jnp.sum(jnp.where(hit_out, local_ids[None, :], 0), axis=1)
    filled = jnp.any(hit_out, axis=1)

    def pack(array):
        blocks = array.reshape(per_dev, BLOCK, head_count, slice_width)
        chosen = jnp.where(filled[:, None, None, None], blocks[pick], jnp.zeros((), array.dtype))
        return chosen.transpose(0, 2, 1, 3).reshape(dev_count, BLOCK, slice_width)

    got = (
        lax.all_to_all(pack(queries), ("seq", "head"), split_axis=0, concat_axis=0, tiled=True),
        lax.all_to_all(pack(keys), ("seq", "head"), split_axis=0, concat_axis=0, tiled=True),
        lax.all_to_all(pack(values), ("seq", "head"), split_axis=0, concat_axis=0, tiled=True),
    )
    hit_in = dev_dest == group_idx
    place = jnp.sum(jnp.where(hit_in, dev_slot, 0), axis=1)
    arrived = jnp.any(hit_in, axis=1)
    owner = owner_of(place, arrived, group_blocks)

    def unpack(array):
        return array[owner].reshape(group_rows, slice_width)

    result_rows = attend(unpack(got[0]), unpack(got[1]), unpack(got[2]), my_lens)
    out_blocks = result_rows.reshape(group_blocks, BLOCK, slice_width)
    bundle = jnp.where(arrived[:, None, None], out_blocks[place], jnp.zeros((), jnp.bfloat16))
    returned = lax.all_to_all(bundle, ("seq", "head"), split_axis=0, concat_axis=0, tiled=True)
    grid = returned.reshape(seq_count, head_count, BLOCK, slice_width)
    mine_back = grid[mine]
    return mine_back.transpose(0, 2, 1, 3).reshape(rows_dev, width)


def solution(mesh):
    placed = (
        P(("seq", "head"), None),
        P(("seq", "head"), None),
        P(("seq", "head"), None),
        P(),
        P(),
    )
    return jax.shard_map(
        local, mesh=mesh, in_specs=placed, out_specs=P(("seq", "head"), None), check_vma=False
    )
```

profile of v0, /device:TPU:1, one launch (start us, length us, event | category | flops | bytes accessed | tf_op | source)
XLA Modules:
  0.0 559.5 jit_solution(6093917833149916626)
XLA Ops:
  0.0 0.8 reshape.369
  1.2 1.5 copy.75
  2.7 1.5 copy.76
  4.2 4.5 gather_fusion.2
  8.8 4.5 gather_fusion.4
  13.3 0.3 copy.74
  13.6 4.5 gather_fusion
  18.1 16.6 %select_bitcast_fusion.2 = (bf16[16,8,128,256]{3,1,2,0:T(8,128)(2,1)}, bf16[16,8,128,256]{3,1,2,0:T(8,128)(2,1)}, bf16[16,8,128,256]{3,1,2,0:T(8,128)(2,1)}) fusion(bf16[16,128,8,256]{3,2,1,0:T(8,128)(2,1)} %gather_fusion, pred[16]{0:T(512)(128)(4,1)S(1)} %fusion.77, bf16[16,128,8,256]{3,2,1,0:T(8,128)(2,1)} %gather_fusion.2, ...), kind=kLoop, calls=%fused_computation.17 | loop fusion | flops 12582912 | bytes 50331664 | tf_op jit(solution)/shard_map/jit(_where)/select_n | solution.py:83
  34.7 9.1 %copy.46 = bf16[16,8,128,256]{3,2,1,0:T(8,128)(2,1)} copy(bf16[16,8,128,256]{3,1,2,0:T(8,128)(2,1)} %get-tuple-element.18) | data formatting | bytes 16777216 | tf_op jit(solution)/shard_map/jit(_where)/select_n | solution.py:83
  43.7 12.0 %all-to-all-start.2 = ((bf16[128,128,256]{2,1,0:T(8,128)(2,1)}), bf16[128,128,256]{2,1,0:T(8,128)(2,1)}, u32[]{:S(2)}, u32[]{:S(2)}) async-start(bf16[128,128,256]{2,1,0:T(8,128)(2,1)} %bitcast.64), calls=%async_computation.2 | async-start | bytes 16777216 | tf_op jit(solution)/shard_map/all_to_all | solution.py:88
  55.7 9.1 %copy.43 = bf16[16,8,128,256]{3,2,1,0:T(8,128)(2,1)} copy(bf16[16,8,128,256]{3,1,2,0:T(8,128)(2,1)} %get-tuple-element.16) | data formatting | bytes 16777216 | tf_op jit(solution)/shard_map/jit(_where)/select_n | solution.py:83
  64.8 91.6 %all-to-all-done.2 = bf16[128,128,256]{2,1,0:T(8,128)(2,1)} async-done(((bf16[128,128,256]{2,1,0:T(8,128)(2,1)}), bf16[128,128,256]{2,1,0:T(8,128)(2,1)}, u32[]{:S(2)}, u32[]{:S(2)}) %all-to-all-start.2) | async-done | bytes 8388640 | tf_op jit(solution)/shard_map/all_to_all | solution.py:88
  156.4 9.4 %all-to-all-start = ((bf16[128,128,256]{2,1,0:T(8,128)(2,1)}), bf16[128,128,256]{2,1,0:T(8,128)(2,1)}, u32[]{:S(2)}, u32[]{:S(2)}) async-start(bf16[128,128,256]{2,1,0:T(8,128)(2,1)} %bitcast.63), calls=%async_computation | async-start | bytes 16777216 | tf_op jit(solution)/shard_map/all_to_all | solution.py:89
  165.9 9.1 %copy.45 = bf16[16,8,128,256]{3,2,1,0:T(8,128)(2,1)} copy(bf16[16,8,128,256]{3,1,2,0:T(8,128)(2,1)} %get-tuple-element.17) | data formatting | bytes 16777216 | tf_op jit(solution)/shard_map/jit(_where)/select_n | solution.py:83
  174.9 91.6 %all-to-all-done = bf16[128,128,256]{2,1,0:T(8,128)(2,1)} async-done(((bf16[128,128,256]{2,1,0:T(8,128)(2,1)}), bf16[128,128,256]{2,1,0:T(8,128)(2,1)}, u32[]{:S(2)}, u32[]{:S(2)}) %all-to-all-start) | async-done | bytes 8388640 | tf_op jit(solution)/shard_map/all_to_all | solution.py:89
  266.6 9.4 %all-to-all-start.1 = ((bf16[128,128,256]{2,1,0:T(8,128)(2,1)}), bf16[128,128,256]{2,1,0:T(8,128)(2,1)}, u32[]{:S(2)}, u32[]{:S(2)}) async-start(bf16[128,128,256]{2,1,0:T(8,128)(2,1)} %bitcast.62), calls=%async_computation.1 | async-start | bytes 16777216 | tf_op jit(solution)/shard_map/all_to_all | solution.py:87
  276.0 0.2 dynamic-slice_reduce_fusion
  276.2 0.2 reduce-window.8
  276.8 1.0 compare_and_fusion.2
  277.9 1.3 compare_and_fusion.1
  279.1 2.2 fusion.8
  281.3 1.6 compare_and_fusion
  282.9 4.0 gather_fusion.5
  286.9 0.8 slice.149
  287.6 4.0 gather_fusion.1
  291.7 0.8 slice.146
  292.4 0.8 slice.150
  293.3 0.3 reshape.451
  293.5 1.1 reshape_reshape.7
  294.7 82.0 %all-to-all-done.1 = bf16[128,128,256]{2,1,0:T(8,128)(2,1)} async-done(((bf16[128,128,256]{2,1,0:T(8,128)(2,1)}), bf16[128,128,256]{2,1,0:T(8,128)(2,1)}, u32[]{:S(2)}, u32[]{:S(2)}) %all-to-all-start.1) | async-done | bytes 8388640 | tf_op jit(solution)/shard_map/all_to_all | solution.py:87
  376.7 5.1 gather_fusion.3
  381.8 2.2 fusion.96
  383.9 1.8 slice.103
  385.7 1.7 slice.105
  387.4 1.7 reshape.448
  389.2 1.0 slice.113
  390.2 0.9 reshape.450
  391.1 2.0 reshape.449
  393.1 1.0 slice.123
  394.1 1.1 slice.125
  395.2 1.1 slice.117
  396.3 1.0 slice.129
  397.3 1.8 fusion.39
  399.1 5.3 fusion.104
  404.4 2.4 fusion.99
  406.8 5.2 fusion.22
  412.0 1.3 fusion.24
  413.3 6.1 %fusion.98 = (f32[2,512]{1,0:T(2,128)S(1)}, f32[2,512,2048]{2,1,0:T(8,128)}) fusion(f32[2,512,2048]{2,1,0:T(8,128)S(1)} %fusion.24, pred[512,2048]{1,0:T(8,128)(4,1)S(1)} %copy-done.5), kind=kOutput, calls=%fused_computation.131 | output fusion | flops 12584959 | bytes 17829888 | tf_op jit(solution)/shard_map/sub | solution.py:41
  419.4 2.3 fusion.105
  421.8 2.1 convolution_convert_fusion
  423.9 0.7 copy-done.15
  424.6 1.0 fusion.21
  425.6 0.3 slice-done.3
  425.9 0.4 copy-done.6
  426.3 1.3 slice-done.4
  427.6 1.7 fusion.23
  429.4 0.5 copy.61
  429.9 6.3 %gather_fusion.6 = bf16[128,128,256]{2,1,0:T(8,128)(2,1)} fusion(bf16[16,128,256]{2,1,0:T(8,128)(2,1)S(1)} %bitcast.59, s32[1024]{0:T(1024)S(1)} %pad_clamp_fusion.1), kind=kCustom, calls=%fused_computation.6 | custom fusion | bytes 16777728 | tf_op jit(solution)/shard_map/gather | solution.py:101
  436.3 7.2 %broadcast_select_fusion = bf16[128,128,256]{2,1,0:T(8,128)(2,1)} fusion(bf16[128,128,256]{2,1,0:T(8,128)(2,1)} %gather_fusion.6, pred[128]{0:T(512)(128)(4,1)S(1)} %get-tuple-element.5), kind=kLoop, calls=%fused_computation.18 | loop fusion | flops 4194304 | bytes 16777344 | tf_op jit(solution)/shard_map/jit(_where)/select_n | solution.py:101
  443.5 9.4 %all-to-all-start.3 = ((bf16[128,128,256]{2,1,0:T(8,128)(2,1)}), bf16[128,128,256]{2,1,0:T(8,128)(2,1)}, u32[]{:S(2)}, u32[]{:S(2)}) async-start(bf16[128,128,256]{2,1,0:T(8,128)(2,1)} %broadcast_select_fusion), calls=%async_computation.3 | async-start | bytes 16777216 | tf_op jit(solution)/shard_map/all_to_all | solution.py:102
  453.0 100.7 %all-to-all-done.3 = bf16[128,128,256]{2,1,0:T(8,128)(2,1)} async-done(((bf16[128,128,256]{2,1,0:T(8,128)(2,1)}), bf16[128,128,256]{2,1,0:T(8,128)(2,1)}, u32[]{:S(2)}, u32[]{:S(2)}) %all-to-all-start.3) | async-done | bytes 8388640 | tf_op jit(solution)/shard_map/all_to_all | solution.py:102
  553.6 4.0 gather_fusion.7
  557.6 0.6 copy.62
  558.2 1.3 copy.77
  (63 shorter events, 0.9 us)
Async XLA Ops:
  0.0 276.0 %copy-start = (s32[16,3]{0,1:T(4,128)S(1)}, s32[16,3]{0,1:T(4,128)}, u32[]{:S(2)}) copy-start(s32[16,3]{0,1:T(4,128)} %param.8) | copy-start | bytes 580
  8.7 4.5 copy-start.4
  43.7 112.7 %all-to-all-start.2 = ((bf16[128,128,256]{2,1,0:T(8,128)(2,1)}), bf16[128,128,256]{2,1,0:T(8,128)(2,1)}, u32[]{:S(2)}, u32[]{:S(2)}) async-start(bf16[128,128,256]{2,1,0:T(8,128)(2,1)} %bitcast.64), calls=%async_computation.2 | async-start | bytes 16777216 | tf_op jit(solution)/shard_map/all_to_all | solution.py:88
  156.4 110.1 %all-to-all-start = ((bf16[128,128,256]{2,1,0:T(8,128)(2,1)}), bf16[128,128,256]{2,1,0:T(8,128)(2,1)}, u32[]{:S(2)}, u32[]{:S(2)}) async-start(bf16[128,128,256]{2,1,0:T(8,128)(2,1)} %bitcast.63), calls=%async_computation | async-start | bytes 16777216 | tf_op jit(solution)/shard_map/all_to_all | solution.py:89
  266.6 110.1 %all-to-all-start.1 = ((bf16[128,128,256]{2,1,0:T(8,128)(2,1)}), bf16[128,128,256]{2,1,0:T(8,128)(2,1)}, u32[]{:S(2)}, u32[]{:S(2)}) async-start(bf16[128,128,256]{2,1,0:T(8,128)(2,1)} %bitcast.62), calls=%async_computation.1 | async-start | bytes 16777216 | tf_op jit(solution)/shard_map/all_to_all | solution.py:87
  286.9 7.8 %copy-start.2 = (bf16[16,128,256]{2,1,0:T(8,128)(2,1)}, bf16[16,128,256]{2,1,0:T(8,128)(2,1)S(1)}, u32[]{:S(2)}) copy-start(bf16[16,128,256]{2,1,0:T(8,128)(2,1)S(1)} %gather_fusion.5) | copy-start | bytes 3145732
  291.6 92.3 %copy-start.3 = (bf16[16,128,256]{2,1,0:T(8,128)(2,1)}, bf16[16,128,256]{2,1,0:T(8,128)(2,1)S(1)}, u32[]{:S(2)}) copy-start(bf16[16,128,256]{2,1,0:T(8,128)(2,1)S(1)} %gather_fusion.1) | copy-start | bytes 3145732
  376.7 13.5 %slice-start = ((bf16[16,128,256]{2,1,0:T(8,128)(2,1)}), bf16[8,128,256]{2,1,0:T(8,128)(2,1)S(1)}, s32[]{:S(2)}) async-start(bf16[16,128,256]{2,1,0:T(8,128)(2,1)} %copy-done.2), calls=%async_computation.4 | async-start | bytes 1048576 | tf_op jit(solution)/shard_map/slice | solution.py:31
  376.7 17.4 %slice-start.1 = ((bf16[16,128,256]{2,1,0:T(8,128)(2,1)}), bf16[12,128,256]{2,1,0:T(8,128)(2,1)S(1)}, s32[]{:S(2)}) async-start(bf16[16,128,256]{2,1,0:T(8,128)(2,1)} %copy-done.2), calls=%async_computation.5 | async-start | bytes 1572864 | tf_op jit(solution)/shard_map/slice | solution.py:31
  383.9 11.2 %slice-start.2 = ((bf16[16,128,256]{2,1,0:T(8,128)(2,1)}), bf16[12,128,256]{2,1,0:T(8,128)(2,1)S(1)}, s32[]{:S(2)}) async-start(bf16[16,128,256]{2,1,0:T(8,128)(2,1)} %copy-done.3), calls=%async_computation.6 | async-start | bytes 1572864 | tf_op jit(solution)/shard_map/slice | solution.py:44
  399.1 5.3 copy-start.7
  399.1 5.3 copy-start.8
  412.0 1.3 copy-start.5
  413.3 6.1 %copy-start.10 = (pred[512,512]{0,1:T(8,128)(4,1)S(1)}, pred[512,512]{0,1:T(8,128)(4,1)}, u32[]{:S(2)}) copy-start(pred[512,512]{0,1:T(8,128)(4,1)} %compare_and_fusion.2) | copy-start | bytes 786436
  413.3 6.1 %copy-start.11 = (bf16[512,2,128]{2,1,0:T(2,128)(2,1)S(1)}, bf16[512,2,128]{2,1,0:T(2,128)(2,1)}, u32[]{:S(2)}) copy-start(bf16[512,2,128]{2,1,0:T(2,128)(2,1)} %slice.103) | copy-start | bytes 786436
  413.3 6.1 %copy-start.13 = (bf16[512,2,128]{2,1,0:T(2,128)(2,1)S(1)}, bf16[512,2,128]{2,1,0:T(2,128)(2,1)}, u32[]{:S(2)}) copy-start(bf16[512,2,128]{2,1,0:T(2,128)(2,1)} %slice.105) | copy-start | bytes 786436
  413.3 8.4 %copy-start.12 = (bf16[512,2,128]{2,1,0:T(2,128)(2,1)S(1)}, bf16[512,2,128]{2,1,0:T(2,128)(2,1)}, u32[]{:S(2)}) copy-start(bf16[512,2,128]{2,1,0:T(2,128)(2,1)} %reshape.448) | copy-start | bytes 786436
  419.4 4.4 copy-start.9
  421.8 2.8 copy-start.15
  421.8 4.1 slice-start.3
  424.6 1.7 copy-start.6
  424.6 3.0 slice-start.4
  427.6 1.7 copy-start.14
  443.5 110.1 %all-to-all-start.3 = ((bf16[128,128,256]{2,1,0:T(8,128)(2,1)}), bf16[128,128,256]{2,1,0:T(8,128)(2,1)}, u32[]{:S(2)}, u32[]{:S(2)}) async-start(bf16[128,128,256]{2,1,0:T(8,128)(2,1)} %broadcast_select_fusion), calls=%async_computation.3 | async-start | bytes 16777216 | tf_op jit(solution)/shard_map/all_to_all | solution.py:102
  452.9 106.6 %copy-start.1 = (s32[16,3]{0,1:T(4,128)S(1)}, s32[16,3]{0,1:T(4,128)}, u32[]{:S(2)}) copy-start(s32[16,3]{0,1:T(4,128)} %param.8) | copy-start | bytes 580
where the time goes:
time: 562 us; the launch traced here: 559 us
  waiting for transfers between devices  366 us (65%)
  local copies, waits for them, and re-layouts  92.9 us (17%)
  other arithmetic  42.2 us (8%)
  starting transfers between devices  40.3 us (7%)
  matrix products  17.7 us (3%)
    all_to_all x1, waiting for transfers between devices, local(): lax.all_to_all(bundle, ('seq', 'head'), split_axis=0, concat_axis=0, tile...  101 us
    all_to_all x1, waiting for transfers between devices, local(): lax.all_to_all(pack(keys), ('seq', 'head'), split_axis=0, concat_axis=0,...  91.6 us
    all_to_all x1, waiting for transfers between devices, local(): lax.all_to_all(pack(values), ('seq', 'head'), split_axis=0, concat_axis=0...  91.6 us
    all_to_all x1, waiting for transfers between devices, local(): lax.all_to_all(pack(queries), ('seq', 'head'), split_axis=0, concat_axis=...  82 us
    select_n x3, local copies, waits for them, and re-layouts, pack(): jnp.where(filled[:, None, None, None], blocks[pick], jnp.zeros((), array....  27.2 us
    select_n x1, other arithmetic, pack(): jnp.where(filled[:, None, None, None], blocks[pick], jnp.zeros((), array....  16.6 us
    gather x3, local copies, waits for them, and re-layouts, pack(): blocks[pick]  13.5 us
    gather x3, local copies, waits for them, and re-layouts, unpack(): return array[owner].reshape(group_rows, slice_width)  13.1 us
  transfers between devices with their start and end apart: 4, of which 4 were waited for; matrix products, arithmetic and copies ran while one was open for 7% of the time, Pallas kernels for 0%

commit v1 on v0

v1 whole, which is shorter than its diff:
```python
import functools
import math

import jax
import jax.numpy as jnp
from jax import lax
from jax.experimental import pallas as pl
from jax.experimental.pallas import tpu as pltpu
from jax.sharding import PartitionSpec as P

HEAD_DIM = 128
BLOCK = 128
SIDE = 4
SEQ = 16
HEAD = 8
BPG = 16
CAP = 2
LONGEST = 10
HEADS_HERE = 2
PAD = LONGEST - 1
WINDOW = LONGEST * BLOCK
MESH = pl.DeviceIdType.MESH
SCALE = 1.0 / math.sqrt(HEAD_DIM)
LOG2E = 1.4426950408889634

ORDER = (
    (1, 0), (0, 1), (3, 0), (0, 3), (2, 0), (0, 2), (1, 1), (3, 3),
    (1, 3), (3, 1), (2, 1), (1, 2), (2, 3), (3, 2), (2, 2),
)
CHUNKS = ((1, 0), (0, 0), (2, 0), (1, 1), (0, 1), (2, 1))
PACK, PLACE, REPACK, RETURN = 0, 32, 48, 80


def tables(plan, group):
    grid = plan.reshape(SEQ, BPG)
    dest, slot = grid // BPG, grid % BPG
    ids = jnp.arange(BPG, dtype=jnp.int32)
    same = (dest[:, :, None] == dest[:, None, :]) & (ids[None, None, :] < ids[None, :, None])
    rank = jnp.sum(same.astype(jnp.int32), axis=2)
    source = jnp.arange(SEQ, dtype=jnp.int32)[:, None]
    offset = ((dest // SIDE - source // SIDE) % SIDE) * SIDE + (dest % SIDE - source % SIDE) % SIDE
    cell = offset * CAP + rank
    cells = jnp.arange(SEQ * CAP, dtype=jnp.int32)
    my_cell = lax.dynamic_index_in_dim(cell, group, 0, keepdims=False)
    pack = jnp.sum(jnp.where(my_cell[None, :] == cells[:, None], ids[None, :], 0), axis=1)
    here = (dest == group).reshape(1, -1)
    flat_cell, flat_slot = cell.reshape(1, -1), slot.reshape(1, -1)
    place = jnp.sum(jnp.where(here & (flat_slot == ids[:, None]), flat_cell, 0), axis=1)
    repack = jnp.sum(jnp.where(here & (flat_cell == cells[:, None]), flat_slot, 0), axis=1)
    return jnp.concatenate([pack, place, repack, my_cell]).astype(jnp.int32)


def kernel(table, lengths, q_in, k_in, v_in, out, *scratch):
    zbuf, xbuf = scratch[0:6], scratch[6:12]
    pbuf, obuf, rbuf = scratch[12], scratch[13:15], scratch[15:17]
    opack, zpack, qg, kg, vg = scratch[17:22]
    z_send, z_recv, z_own, x_send, x_recv, y_send, y_recv, w_send, w_recv, w_own = scratch[22:]
    inputs = (q_in, k_in, v_in)
    s = lax.axis_index("seq")
    h = lax.axis_index("head")
    y, x = s // SIDE, s % SIDE

    def across(dx, dy):
        return (((y + dy) % SIDE) * SIDE + (x + dx) % SIDE, h)

    def peer(step):
        return lax.rem(h + step, HEAD)

    barrier = pltpu.get_barrier_semaphore()
    for dx, dy in ORDER:
        pl.semaphore_signal(barrier, inc=1, device_id=across(dx, dy), device_id_type=MESH)
    for step in range(1, HEAD):
        pl.semaphore_signal(barrier, inc=1, device_id=(s, peer(step)), device_id_type=MESH)
    pl.semaphore_wait(barrier, len(ORDER) + HEAD - 1)

    def z_copy(c, step):
        tensor, head = CHUNKS[c]
        to = peer(step)
        column = pl.multiple_of((to * HEADS_HERE + head) * HEAD_DIM, HEAD_DIM)
        return pltpu.make_async_remote_copy(
            src_ref=inputs[tensor].at[:, :, pl.ds(column, HEAD_DIM)],
            dst_ref=zbuf[c].at[pl.ds(h * CAP, CAP)],
            send_sem=z_send.at[c, step],
            recv_sem=z_recv.at[c, step],
            device_id=(s, to),
            device_id_type=MESH,
        )

    def z_local(c):
        tensor, head = CHUNKS[c]
        column = pl.multiple_of((h * HEADS_HERE + head) * HEAD_DIM, HEAD_DIM)
        return pltpu.make_async_copy(
            inputs[tensor].at[:, :, pl.ds(column, HEAD_DIM)],
            zbuf[c].at[pl.ds(h * CAP, CAP)],
            z_own.at[c],
        )

    def z_start(c):
        for step in range(1, HEAD):
            z_copy(c, step).start()
        z_local(c).start()

    def z_wait(c):
        z_local(c).wait()
        for step in range(1, HEAD):
            z_copy(c, step).wait_recv()

    def x_copy(c, dx, dy):
        offset = dy * SIDE + dx
        return pltpu.make_async_remote_copy(
            src_ref=pbuf.at[c, offset],
            dst_ref=xbuf[c].at[pl.ds(offset * CAP, CAP)],
            send_sem=x_send.at[c, offset],
            recv_sem=x_recv.at[c, offset],
            device_id=across(dx, dy),
            device_id_type=MESH,
        )

    def rows_of(index):
        return pl.ds(pl.multiple_of(index * BLOCK, BLOCK), BLOCK)

    def x_start(c):
        for dx, dy in ORDER:
            offset = dy * SIDE + dx
            for j in range(CAP):
                pbuf[c, offset, j] = zbuf[c][table[PACK + offset * CAP + j]]
            x_copy(c, dx, dy).start()
        for j in range(CAP):
            xbuf[c][j] = zbuf[c][table[PACK + j]]

    def x_wait(c):
        for dx, dy in ORDER:
            x_copy(c, dx, dy).wait_recv()

    first_end = lengths[s, 0]
    second_end = first_end + lengths[s, 1]

    def attend(head):
        k_chunk, q_chunk, v_chunk = (xbuf[3 * head + i] for i in range(3))

        def gather(r, carry):
            index = table[PLACE + r]
            rows, padded = rows_of(r), rows_of(r + PAD)
            qg[rows] = q_chunk[index]
            kg[padded] = k_chunk[index]
            vg[padded, :HEAD_DIM] = v_chunk[index]
            return carry

        lax.fori_loop(0, BPG, gather, 0)
        behind = lax.broadcasted_iota(jnp.int32, (1, WINDOW), 1) // BLOCK - PAD

        def record(index):
            return (index >= first_end).astype(jnp.int32) + (index >= second_end).astype(jnp.int32)

        down = lax.broadcasted_iota(jnp.int32, (BLOCK, BLOCK), 0)
        along = lax.broadcasted_iota(jnp.int32, (BLOCK, BLOCK), 1)
        corner = jnp.where(along <= down, 0.0, -1e30).astype(jnp.float32)

        def block(i, carry):
            theirs = behind + i
            seen = (record(theirs) == record(jnp.full_like(theirs, i))) & (theirs >= 0)
            bias = jnp.where(seen, 0.0, -1e30).astype(jnp.float32)
            window = pl.ds(pl.multiple_of(i * BLOCK, BLOCK), WINDOW)
            scores = lax.dot_general(
                qg[rows_of(i)], kg[window], (((1,), (1,)), ((), ())), preferred_element_type=jnp.float32
            )
            scores = jnp.concatenate(
                [scores[:, : WINDOW - BLOCK] + bias[:, : WINDOW - BLOCK], scores[:, WINDOW - BLOCK :] + corner], axis=1
            )
            peak = jnp.max(scores, axis=1, keepdims=True)
            weights = jnp.exp2((scores - peak) * (SCALE * LOG2E)).astype(jnp.bfloat16)
            both = jnp.dot(weights, vg[window], preferred_element_type=jnp.float32)
            obuf[head][i] = (both[:, :HEAD_DIM] / both[:, HEAD_DIM:]).astype(jnp.bfloat16)
            return carry

        lax.fori_loop(0, BPG, block, 0)

    def y_copy(head, dx, dy):
        offset = dy * SIDE + dx
        return pltpu.make_async_remote_copy(
            src_ref=opack.at[head, offset],
            dst_ref=rbuf[head].at[pl.ds(offset * CAP, CAP)],
            send_sem=y_send.at[head, offset],
            recv_sem=y_recv.at[head, offset],
            device_id=across(SIDE - dx, SIDE - dy),
            device_id_type=MESH,
        )

    def y_start(head):
        for dx, dy in ORDER:
            offset = dy * SIDE + dx
            for j in range(CAP):
                opack[head, offset, j] = obuf[head][table[REPACK + offset * CAP + j]]
            y_copy(head, dx, dy).start()
        for j in range(CAP):
            rbuf[head][j] = obuf[head][table[REPACK + j]]

    def w_copy(head, step):
        to = peer(step)
        column = pl.multiple_of((h * HEADS_HERE + head) * HEAD_DIM, HEAD_DIM)
        return pltpu.make_async_remote_copy(
            src_ref=zpack.at[head, to],
            dst_ref=out.at[:, :, pl.ds(column, HEAD_DIM)],
            send_sem=w_send.at[head, step],
            recv_sem=w_recv.at[head, step],
            device_id=(s, to),
            device_id_type=MESH,
        )

    def w_local(head):
        column = pl.multiple_of((h * HEADS_HERE + head) * HEAD_DIM, HEAD_DIM)
        return pltpu.make_async_copy(
            zpack.at[head, h], out.at[:, :, pl.ds(column, HEAD_DIM)], w_own.at[head]
        )

    def w_start(head):
        for dx, dy in ORDER:
            y_copy(head, dx, dy).wait_recv()
        for step in range(1, HEAD + 1):
            to = peer(step)
            for j in range(CAP):
                zpack[head, to, j] = rbuf[head][table[RETURN + to * CAP + j]]
            if step < HEAD:
                w_copy(head, step).start()
            else:
                w_local(head).start()

    z_start(0)
    z_start(1)
    kg[: PAD * BLOCK] = jnp.zeros((PAD * BLOCK, HEAD_DIM), jnp.bfloat16)
    vg[: PAD * BLOCK, :HEAD_DIM] = jnp.zeros((PAD * BLOCK, HEAD_DIM), jnp.bfloat16)
    vg[:, HEAD_DIM:] = jnp.ones(((PAD + BPG) * BLOCK, HEAD_DIM), jnp.bfloat16)
    for c in range(6):
        z_wait(c)
        x_start(c)
        if c + 2 < 6:
            z_start(c + 2)
    for head in range(HEADS_HERE):
        for c in range(3 * head, 3 * head + 3):
            x_wait(c)
        attend(head)
        y_start(head)
    for head in range(HEADS_HERE):
        w_start(head)
    for head in range(HEADS_HERE):
        w_local(head).wait()
        for step in range(1, HEAD):
            w_copy(head, step).wait()
        for dx, dy in ORDER:
            y_copy(head, dx, dy).wait_send()
    for c in range(6):
        for step in range(1, HEAD):
            z_copy(c, step).wait_send()
        for dx, dy in ORDER:
            x_copy(c, dx, dy).wait_send()


def local(queries, keys, values, lengths, plan):
    table = tables(plan, lax.axis_index("seq"))
    queries, keys, values = (array.reshape(CAP, BLOCK, -1) for array in (queries, keys, values))
    bf16 = jnp.bfloat16
    attended = pl.pallas_call(
        kernel,
        out_shape=jax.ShapeDtypeStruct(queries.shape, bf16),
        in_specs=[pl.BlockSpec(memory_space=pltpu.SMEM)] * 2 + [pl.BlockSpec(memory_space=pl.ANY)] * 3,
        out_specs=pl.BlockSpec(memory_space=pl.ANY),
        scratch_shapes=[pltpu.VMEM((BPG, BLOCK, HEAD_DIM), bf16)] * 6
        + [pltpu.VMEM((SEQ * CAP, BLOCK, HEAD_DIM), bf16)] * 6
        + [pltpu.VMEM((6, SEQ, CAP, BLOCK, HEAD_DIM), bf16)]
        + [pltpu.VMEM((BPG, BLOCK, HEAD_DIM), bf16)] * 2
        + [pltpu.VMEM((SEQ * CAP, BLOCK, HEAD_DIM), bf16)] * 2
        + [
            pltpu.VMEM((HEADS_HERE, SEQ, CAP, BLOCK, HEAD_DIM), bf16),
            pltpu.VMEM((HEADS_HERE, HEAD, CAP, BLOCK, HEAD_DIM), bf16),
            pltpu.VMEM((BPG * BLOCK, HEAD_DIM), bf16),
            pltpu.VMEM(((PAD + BPG) * BLOCK, HEAD_DIM), bf16),
            pltpu.VMEM(((PAD + BPG) * BLOCK, 2 * HEAD_DIM), bf16),
            pltpu.SemaphoreType.DMA((6, HEAD)),
            pltpu.SemaphoreType.DMA((6, HEAD)),
            pltpu.SemaphoreType.DMA((6,)),
            pltpu.SemaphoreType.DMA((6, SEQ)),
            pltpu.SemaphoreType.DMA((6, SEQ)),
            pltpu.SemaphoreType.DMA((HEADS_HERE, SEQ)),
            pltpu.SemaphoreType.DMA((HEADS_HERE, SEQ)),
            pltpu.SemaphoreType.DMA((HEADS_HERE, HEAD)),
            pltpu.SemaphoreType.DMA((HEADS_HERE, HEAD)),
            pltpu.SemaphoreType.DMA((HEADS_HERE,)),
        ],
        compiler_params=pltpu.CompilerParams(
            collective_id=0, has_side_effects=True, vmem_limit_bytes=44 * 2**20
        ),
        cost_estimate=pl.CostEstimate(flops=2_000_000_000, bytes_accessed=4 * 2**20, transcendentals=4_000_000),
    )(table, lengths, queries, keys, values)
    return attended.reshape(CAP * BLOCK, -1)


def solution(mesh):
    placed = (
        P(("seq", "head"), None),
        P(("seq", "head"), None),
        P(("seq", "head"), None),
        P(),
        P(),
    )
    return jax.shard_map(
        local, mesh=mesh, in_specs=placed, out_specs=P(("seq", "head"), None), check_vma=False
    )
```

time: 562 us -> 137 us (0.24)
  waiting for transfers between devices: 366 us -> 0 us
  Pallas kernels: 0 us -> 129 us
  local copies, waits for them, and re-layouts: 92.9 us -> 6.48 us
  other arithmetic: 42.2 us -> 1.06 us
  starting transfers between devices: 40.3 us -> 0 us
  matrix products: 17.7 us -> 0 us
    all_to_all x4 -> x0, waiting for transfers between devices: 366 us -> none  [the longest x1 101 us: local(): lax.all_to_all(bundle, ('seq', 'head'), split_axis=0, concat_axis=0, tile...]
    pallas_call x0 -> x1, Pallas kernels: none -> 129 us  [local(): pl.pallas_call(kernel, out_shape=jax.ShapeDtypeStruct(queries.shape, bf16...]
    all_to_all x4 -> x0, starting transfers between devices: 40.3 us -> none  [the longest x1 12 us: local(): lax.all_to_all(pack(keys), ('seq', 'head'), split_axis=0, concat_axis=0,...]
    gather x8 -> x0, local copies, waits for them, and re-layouts: 36.9 us -> none  [the longest x3 13.5 us: pack(): blocks[pick]]
    select_n x3 -> x0, local copies, waits for them, and re-layouts: 27.2 us -> none  [pack(): jnp.where(filled[:, None, None, None], blocks[pick], jnp.zeros((), array....]
    select_n x6 -> x3, other arithmetic: 23.8 us -> 0.03 us  [the longest x1 0.02 us: tables(): dest, slot = (grid // BPG, grid % BPG)]
    slice x21 -> x0, local copies, waits for them, and re-layouts: 17.9 us -> none  [the longest x5 6.98 us: attend(): q_three[start:stop]]
    dot_general x6 -> x0, matrix products: 13 us -> none  [the longest x4 9.95 us: attend(): jnp.einsum('hqk,khd->qhd', weights, v_three[:stop], preferred_element_typ...]
  transfers between devices with their start and end apart: 4 -> 0, of which waited for: 4 -> 0; matrix products, arithmetic and copies ran while one was open for 7% -> 0% of each run, Pallas kernels for 0% -> 0%
where the time goes in v1:
time: 137 us
  Pallas kernels  129 us (94%)
  local copies, waits for them, and re-layouts  6.48 us (5%)
    pallas_call x1, Pallas kernels, local(): pl.pallas_call(kernel, out_shape=jax.ShapeDtypeStruct(queries.shape, bf16...  129 us
    unnamed x12, local copies, waits for them, and re-layouts  6.02 us

profile of v1, /device:TPU:1, one launch (start us, length us, event | category | flops | bytes accessed | tf_op | source)
XLA Modules:
  0.0 137.1 jit_solution(15129769174223964797)
XLA Ops:
  0.0 0.0 copy-start.3
  0.0 0.7 copy-done.3
  0.7 0.1 reshape.238
  0.8 0.1 sub.57
  0.9 0.1 sub.63
  0.9 0.1 sub.55
  1.0 0.0 copy-start.4
  1.0 0.1 sub.61
  1.1 0.6 copy-done.4
  1.7 0.1 copy.7.lengths
  1.8 0.1 broadcast_compare_fusion
  1.9 0.1 negate_select_fusion
  2.0 0.4 convert_reduce_fusion
  2.4 0.1 reduce_sum.40
  2.5 0.1 select_reduce_fusion
  2.6 0.1 select_reduce_fusion.1
  2.8 0.1 select_reduce_fusion.2
  2.8 0.1 pad_add_fusion.table
  2.9 0.0 copy-start
  2.9 1.2 copy-done
  4.2 0.0 copy-start.1
  4.2 1.2 copy-done.1
  5.4 0.0 copy-start.2
  5.4 1.2 copy-done.2
  6.6 129.5 %shard_map.55 = bf16[2,128,2048]{2,1,0:T(8,128)(2,1)S(1)} custom-call(s32[96]{0:T(128)S(1)} %pad_add_fusion.table, s32[16,3]{1,0:T(8,128)S(1)} %copy.7.lengths, bf16[2,128,2048]{2,1,0:T(8,128)(2,1)S(1)} %bitcast.7, bf16[2,128,2048]{2,1,0:T(8,128)(2,1)S(1)} %bitcast.8, bf16[2,128,2048]{2,1,0:T(8,128)(2,1)S(1)} %bitcast.9), custom_call_target="tpu_custom_call" | custom-call | flops 2000000000 | bytes 4194304 | tf_op jit(solution)/shard_map/pallas_call | solution.py:262
  136.1 1.0 copy.9
  (7 shorter events, 0.1 us)
Async XLA Ops:
  0.0 0.7 copy-start.3
  1.0 0.7 copy-start.4
  2.9 1.2 copy-start
  4.2 1.2 copy-start.1
  5.4 1.2 copy-start.2

commit v2 on v0

v2 whole, which is shorter than its diff:
```python
import functools
import math

import jax
import jax.numpy as jnp
from jax import lax
from jax.experimental import pallas as pl
from jax.experimental.pallas import tpu as pltpu
from jax.sharding import PartitionSpec as P

HEAD_DIM = 128
BLOCK = 128
SEQ = 16
HEAD = 8
BPG = 16
CAP = 2
LONGEST = 10
HEADS_HERE = 2
PAD = LONGEST - 1
WINDOW = LONGEST * BLOCK
MESH = pl.DeviceIdType.MESH
SCALE = 1.0 / math.sqrt(HEAD_DIM)
LOG2E = 1.4426950408889634
QUERY, KEY, VALUE = 0, 1, 2

COMING = (
    (KEY, 0, 0, 64), (KEY, 0, 64, 64), (QUERY, 0, 0, 128), (VALUE, 0, 0, 128),
    (KEY, 1, 0, 128), (QUERY, 1, 0, 128), (VALUE, 1, 0, 128),
)
GOING = ((0, 0, 128), (1, 0, 64), (1, 64, 64))
AHEAD = 3

LEFT_OUT = ((2, 8, 10), ())


def spots(left_out):
    return tuple(offset for offset in range(1, SEQ) if offset not in left_out)


def serves(plan, left_out):
    offset = (plan // BPG - jnp.arange(plan.shape[0], dtype=jnp.int32) // BPG) % SEQ
    moved = (offset[None, :] - jnp.arange(SEQ, dtype=jnp.int32)[:, None]) % SEQ
    misses = functools.reduce(jnp.logical_or, [moved == one for one in left_out])
    return jnp.min(jnp.sum(misses.astype(jnp.int32), axis=1)) == 0


def fill_tables(left_out, plan, here, columns):
    cells = CAP * (SEQ - len(left_out))
    wide = (1, SEQ * BPG)
    lane = lax.broadcasted_iota(jnp.int32, wide, 1)
    source, ids = lane // BPG, lane % BPG
    dest, slot = plan[...] // BPG, plan[...] % BPG
    straight = (dest - source) % SEQ
    shift = jnp.zeros((1, 1), jnp.int32)
    if left_out:
        tried = lax.broadcasted_iota(jnp.int32, (SEQ, SEQ * BPG), 0)
        moved = (straight - tried) % SEQ
        misses = functools.reduce(jnp.add, [(moved == one).astype(jnp.int32) for one in left_out])
        misses = jnp.sum(misses, axis=1, keepdims=True)
        rows = lax.broadcasted_iota(jnp.int32, (SEQ, 1), 0)
        shift = jnp.min(jnp.where(misses == 0, rows, SEQ - 1), axis=0, keepdims=True)
    rank = jnp.zeros(wide, jnp.int32)
    for back in range(1, BPG):
        earlier = pltpu.roll(dest, back, 1)
        rank = rank + ((earlier == dest) & (ids >= back)).astype(jnp.int32)
    place = (dest - shift) % SEQ
    offset = (straight - shift) % SEQ
    spot = offset
    for one in left_out:
        spot = spot - (offset > one).astype(jnp.int32)
    cell = spot * CAP + rank
    going, coming = source == here, place == here

    def pick(count, chosen, key, value, limit):
        rows = lax.broadcasted_iota(jnp.int32, (count, SEQ * BPG), 0)
        picked = jnp.sum(jnp.where(chosen & (key == rows), value, 0), axis=1, keepdims=True)
        return jnp.minimum(picked, limit - 1)

    found = jnp.concatenate(
        [
            jnp.pad(pick(cells, going, cell, ids, BPG), ((0, SEQ * CAP - cells), (0, 0))),
            pick(BPG, coming, slot, cell, cells),
            jnp.pad(pick(cells, coming, cell, slot, BPG), ((0, SEQ * CAP - cells), (0, 0))),
            pick(BPG, going, ids, cell, cells),
            jnp.broadcast_to(shift, (BLOCK - SHIFT, 1)),
        ],
        axis=0,
    )
    columns[...] = jnp.broadcast_to(found, (BLOCK, BLOCK)).T[:8]


PACK, PLACE, REPACK, RETURN, SHIFT = 0, 32, 48, 80, 96


def kernel(left_out, plan, lengths, q_in, k_in, v_in, out, *scratch):
    scratch = list(scratch)

    def take(count):
        taken, scratch[:] = scratch[:count], scratch[count:]
        return taken

    zbuf, xbuf, pbuf = (take(len(COMING)) for _ in range(3))
    opack, rbuf, zpack = (take(len(GOING)) for _ in range(3))
    obuf = take(HEADS_HERE)
    qg, kg, vg, columns, table, t_sem, z_send, z_recv, x_send, x_recv, y_send, y_recv, w_send, w_recv = scratch
    inputs = (q_in, k_in, v_in)
    offsets = spots(left_out)
    s = lax.axis_index("seq")
    h = lax.axis_index("head")

    def across(offset):
        return (lax.rem(s + offset, SEQ), h)

    def peer(step):
        return lax.rem(h + step, HEAD)

    barrier = pltpu.get_barrier_semaphore()
    partners = sorted({offset for one in offsets for offset in (one, SEQ - one)})
    for step in range(1, HEAD):
        pl.semaphore_signal(barrier, inc=1, device_id=(s, peer(step)), device_id_type=MESH)
    for offset in partners:
        pl.semaphore_signal(barrier, inc=1, device_id=across(offset), device_id_type=MESH)
    fill_tables(left_out, plan, s, columns)
    fetch = pltpu.make_async_copy(columns, table, t_sem)
    fetch.start()
    kg[: PAD * BLOCK] = jnp.zeros((PAD * BLOCK, HEAD_DIM), jnp.bfloat16)
    vg[: PAD * BLOCK, :HEAD_DIM] = jnp.zeros((PAD * BLOCK, HEAD_DIM), jnp.bfloat16)
    vg[:, HEAD_DIM:] = jnp.ones(((PAD + BPG) * BLOCK, HEAD_DIM), jnp.bfloat16)
    pl.semaphore_wait(barrier, len(partners) + HEAD - 1)

    def columns_of(device, head):
        return pl.ds(pl.multiple_of((device * HEADS_HERE + head) * HEAD_DIM, HEAD_DIM), HEAD_DIM)

    def wait_for(ref, sem):
        pltpu.make_async_copy(ref, ref, sem).wait()

    def z_start(u):
        tensor, head, row, rows = COMING[u]
        for step in range(1, HEAD):
            to = peer(step)
            pltpu.make_async_remote_copy(
                src_ref=inputs[tensor].at[:, pl.ds(row, rows), columns_of(to, head)],
                dst_ref=zbuf[u].at[pl.ds(h * CAP, CAP)],
                send_sem=z_send.at[u],
                recv_sem=z_recv.at[u],
                device_id=(s, to),
                device_id_type=MESH,
            ).start()
        pltpu.make_async_copy(
            inputs[tensor].at[:, pl.ds(row, rows), columns_of(h, head)], zbuf[u].at[pl.ds(h * CAP, CAP)], z_recv.at[u]
        ).start()

    def z_wait(u):
        wait_for(zbuf[u], z_recv.at[u])

    def x_start(u):
        for spot, offset in enumerate(offsets):
            for j in range(CAP):
                pbuf[u][spot * CAP + j] = zbuf[u][table[0, PACK + (spot + 1) * CAP + j]]
            pltpu.make_async_remote_copy(
                src_ref=pbuf[u].at[pl.ds(spot * CAP, CAP)],
                dst_ref=xbuf[u].at[pl.ds((spot + 1) * CAP, CAP)],
                send_sem=x_send.at[u],
                recv_sem=x_recv.at[u],
                device_id=across(offset),
                device_id_type=MESH,
            ).start()
        for j in range(CAP):
            xbuf[u][j] = zbuf[u][table[0, PACK + j]]

    def x_wait(u):
        wait_for(xbuf[u].at[pl.ds(CAP, len(offsets) * CAP)], x_recv.at[u])

    def attend(head):
        group = lax.rem(s + table[0, SHIFT], SEQ)
        first_end = lengths[0, group]
        second_end = first_end + lengths[1, group]

        def gather(r, carry):
            index = table[0, PLACE + r]
            for u, (tensor, own, row, rows) in enumerate(COMING):
                if own != head:
                    continue
                ahead = 0 if tensor == QUERY else PAD * BLOCK
                at = pl.ds(pl.multiple_of(r * BLOCK + (ahead + row), rows), rows)
                if tensor == VALUE:
                    vg[at, :HEAD_DIM] = xbuf[u][index]
                else:
                    (qg, kg)[tensor][at] = xbuf[u][index]
            return carry

        lax.fori_loop(0, BPG, gather, 0)
        behind = lax.broadcasted_iota(jnp.int32, (1, WINDOW), 1) // BLOCK - PAD
        down = lax.broadcasted_iota(jnp.int32, (BLOCK, BLOCK), 0)
        along = lax.broadcasted_iota(jnp.int32, (BLOCK, BLOCK), 1)
        corner = jnp.where(along <= down, 0.0, -1e30).astype(jnp.float32)

        def record(index):
            return (index >= first_end).astype(jnp.int32) + (index >= second_end).astype(jnp.int32)

        def block(i, carry):
            theirs = behind + i
            seen = (record(theirs) == record(jnp.full_like(theirs, i))) & (theirs >= 0)
            bias = jnp.where(seen, 0.0, -1e30).astype(jnp.float32)
            rows = pl.ds(pl.multiple_of(i * BLOCK, BLOCK), BLOCK)
            window = pl.ds(pl.multiple_of(i * BLOCK, BLOCK), WINDOW)
            scores = lax.dot_general(
                qg[rows], kg[window], (((1,), (1,)), ((), ())), preferred_element_type=jnp.float32
            )
            scores = jnp.concatenate(
                [scores[:, : WINDOW - BLOCK] + bias[:, : WINDOW - BLOCK], scores[:, WINDOW - BLOCK :] + corner], axis=1
            )
            peak = jnp.max(scores, axis=1, keepdims=True)
            weights = jnp.exp2((scores - peak) * (SCALE * LOG2E)).astype(jnp.bfloat16)
            both = jnp.dot(weights, vg[window], preferred_element_type=jnp.float32)
            obuf[head][i] = (both[:, :HEAD_DIM] / both[:, HEAD_DIM:]).astype(jnp.bfloat16)
            return carry

        lax.fori_loop(0, BPG, block, 0, unroll=4)

    def y_start(w):
        head, row, rows = GOING[w]
        for spot, offset in enumerate(offsets):
            for j in range(CAP):
                opack[w][spot * CAP + j] = obuf[head][table[0, REPACK + (spot + 1) * CAP + j], row : row + rows]
            pltpu.make_async_remote_copy(
                src_ref=opack[w].at[pl.ds(spot * CAP, CAP)],
                dst_ref=rbuf[w].at[pl.ds((spot + 1) * CAP, CAP)],
                send_sem=y_send.at[w],
                recv_sem=y_recv.at[w],
                device_id=across(SEQ - offset),
                device_id_type=MESH,
            ).start()
        for j in range(CAP):
            rbuf[w][j] = obuf[head][table[0, REPACK + j], row : row + rows]

    def w_start(w):
        head, row, rows = GOING[w]
        wait_for(rbuf[w].at[pl.ds(CAP, len(offsets) * CAP)], y_recv.at[w])
        for step in range(1, HEAD + 1):
            to = peer(step)
            for j in range(CAP):
                zpack[w][to, j] = rbuf[w][table[0, RETURN + to * CAP + j]]
            target = out.at[:, pl.ds(row, rows), columns_of(h, head)]
            if step == HEAD:
                pltpu.make_async_copy(zpack[w].at[to], target, w_recv.at[w]).start()
                continue
            pltpu.make_async_remote_copy(
                src_ref=zpack[w].at[to],
                dst_ref=target,
                send_sem=w_send.at[w],
                recv_sem=w_recv.at[w],
                device_id=(s, to),
                device_id_type=MESH,
            ).start()

    for u in range(AHEAD):
        z_start(u)
    fetch.wait()
    for u in range(len(COMING)):
        z_wait(u)
        x_start(u)
        if u + AHEAD < len(COMING):
            z_start(u + AHEAD)
    first = [u for u, unit in enumerate(COMING) if unit[1] == 0]
    second = [u for u, unit in enumerate(COMING) if unit[1] == 1]
    for u in first:
        x_wait(u)
    attend(0)
    for u in second[:-1]:
        x_wait(u)
    y_start(0)
    x_wait(second[-1])
    attend(1)
    for w in range(1, len(GOING)):
        y_start(w)
    for w in range(len(GOING)):
        w_start(w)
    for u in range(len(COMING)):
        wait_for(zbuf[u].at[pl.ds(0, (HEAD - 1) * CAP)], z_send.at[u])
        wait_for(pbuf[u], x_send.at[u])
    for w, (_, row, rows) in enumerate(GOING):
        wait_for(opack[w], y_send.at[w])
        wait_for(zpack[w].at[pl.ds(0, HEAD - 1)], w_send.at[w])
        wait_for(out.at[:, pl.ds(row, rows), pl.ds(0, HEAD * HEAD_DIM)], w_recv.at[w])


def exchange(number, left_out, queries, keys, values, lengths, plan):
    bf16 = jnp.bfloat16
    count = len(spots(left_out))

    def blocks(many, rows):
        return pltpu.VMEM((many, rows, HEAD_DIM), bf16)

    def in_flight(units):
        return pltpu.SemaphoreType.DMA((len(units),))

    return pl.pallas_call(
        functools.partial(kernel, left_out),
        out_shape=jax.ShapeDtypeStruct(queries.shape, bf16),
        in_specs=[pl.BlockSpec(memory_space=pltpu.VMEM), pl.BlockSpec(memory_space=pltpu.SMEM)]
        + [pl.BlockSpec(memory_space=pl.ANY)] * 3,
        out_specs=pl.BlockSpec(memory_space=pl.ANY),
        scratch_shapes=[blocks(BPG, unit[3]) for unit in COMING]
        + [blocks((count + 1) * CAP, unit[3]) for unit in COMING]
        + [blocks(count * CAP, unit[3]) for unit in COMING]
        + [blocks(count * CAP, unit[2]) for unit in GOING]
        + [blocks((count + 1) * CAP, unit[2]) for unit in GOING]
        + [pltpu.VMEM((HEAD, CAP, unit[2], HEAD_DIM), bf16) for unit in GOING]
        + [blocks(BPG, BLOCK)] * HEADS_HERE
        + [
            pltpu.VMEM((BPG * BLOCK, HEAD_DIM), bf16),
            pltpu.VMEM(((PAD + BPG) * BLOCK, HEAD_DIM), bf16),
            pltpu.VMEM(((PAD + BPG) * BLOCK, 2 * HEAD_DIM), bf16),
            pltpu.VMEM((8, BLOCK), jnp.int32),
            pltpu.SMEM((8, BLOCK), jnp.int32),
            pltpu.SemaphoreType.DMA,
        ]
        + [in_flight(COMING)] * 4
        + [in_flight(GOING)] * 4,
        compiler_params=pltpu.CompilerParams(
            collective_id=number, has_side_effects=True, vmem_limit_bytes=63 * 2**20
        ),
        cost_estimate=pl.CostEstimate(flops=2_000_000_000, bytes_accessed=4 * 2**20, transcendentals=4_000_000),
    )(plan.reshape(1, -1), lengths.T, queries, keys, values)


def local(queries, keys, values, lengths, plan):
    queries, keys, values = (array.reshape(CAP, BLOCK, -1) for array in (queries, keys, values))
    forms = [functools.partial(exchange, number, left_out) for number, left_out in enumerate(LEFT_OUT)]
    attended = lax.cond(serves(plan, LEFT_OUT[0]), *forms, queries, keys, values, lengths, plan)
    return attended.reshape(CAP * BLOCK, -1)


def solution(mesh):
    placed = (
        P(("seq", "head"), None),
        P(("seq", "head"), None),
        P(("seq", "head"), None),
        P(),
        P(),
    )
    return jax.shard_map(
        local, mesh=mesh, in_specs=placed, out_specs=P(("seq", "head"), None), check_vma=False
    )
```

time: 562 us -> 103 us (0.18)
  waiting for transfers between devices: 366 us -> 0 us
  Pallas kernels: 0 us -> 98.8 us
  local copies, waits for them, and re-layouts: 92.9 us -> 2.99 us
  other arithmetic: 42.2 us -> 0.78 us
  starting transfers between devices: 40.3 us -> 0 us
  matrix products: 17.7 us -> 0 us
    all_to_all x4 -> x0, waiting for transfers between devices: 366 us -> none  [the longest x1 101 us: local(): lax.all_to_all(bundle, ('seq', 'head'), split_axis=0, concat_axis=0, tile...]
    pallas_call x0 -> x1, Pallas kernels: none -> 98.8 us  [exchange(): pl.pallas_call(functools.partial(kernel, left_out), out_shape=jax.ShapeDt...]
    all_to_all x4 -> x0, starting transfers between devices: 40.3 us -> none  [the longest x1 12 us: local(): lax.all_to_all(pack(keys), ('seq', 'head'), split_axis=0, concat_axis=0,...]
    gather x8 -> x0, local copies, waits for them, and re-layouts: 36.9 us -> none  [the longest x3 13.5 us: pack(): blocks[pick]]
    select_n x3 -> x0, local copies, waits for them, and re-layouts: 27.2 us -> none  [pack(): jnp.where(filled[:, None, None, None], blocks[pick], jnp.zeros((), array....]
    select_n x6 -> x1, other arithmetic: 23.8 us -> 0.02 us  [serves(): (plan // BPG - jnp.arange(plan.shape[0], dtype=jnp.int32) // BPG) % SEQ]
    slice x21 -> x0, local copies, waits for them, and re-layouts: 17.9 us -> none  [the longest x5 6.98 us: attend(): q_three[start:stop]]
    dot_general x6 -> x0, matrix products: 13 us -> none  [the longest x4 9.95 us: attend(): jnp.einsum('hqk,khd->qhd', weights, v_three[:stop], preferred_element_typ...]
  transfers between devices with their start and end apart: 4 -> 0, of which waited for: 4 -> 0; matrix products, arithmetic and copies ran while one was open for 7% -> 0% of each run, Pallas kernels for 0% -> 0%
where the time goes in v2:
time: 103 us
  Pallas kernels  98.8 us (96%)
  local copies, waits for them, and re-layouts  2.99 us (3%)
    pallas_call x1, Pallas kernels, exchange(): pl.pallas_call(functools.partial(kernel, left_out), out_shape=jax.ShapeDt...  98.8 us
    unnamed x5, local copies, waits for them, and re-layouts  2.99 us

profile of v2, /device:TPU:1, one launch (start us, length us, event | category | flops | bytes accessed | tf_op | source)
XLA Modules:
  0.0 103.3 jit_solution(462733276304786044)
XLA Ops:
  0.0 0.0 copy-start
  0.0 0.7 copy-done
  0.7 0.1 convert_reduce_fusion
  0.8 0.0 copy-start.1
  0.8 0.6 reduce_min.9
  2.1 0.0 copy-done.1
  2.1 98.8 %conditional.1 = (bf16[256,2048]{1,0:T(8,128)(2,1)}) conditional(s32[]{:T(128)} %convert_element_type.7, (s32[256]{0:T(256)S(1)}, s32[16,3]{0,1:T(4,128)S(1)}, bf16[2,128,2048]{2,1,0:T(8,128)(2,1)}, bf16[2,128,2048]{2,1,0:T(8,128)(2,1)}, bf16[2,128,2048]{2,1,0:T(8,128)(2,1)}) %tuple.26, (s32[256]{0:T(256)S(1)}, s32[16,3]{0,1:T(4,128)S(1)}, ...), branch_computations={%region_2.3_spmd, %region_3.4_spmd} | conditional | flops 2000000000 | bytes 4194312 | solution.py:331
  2.1 98.8 %branch_1_fun.1 = bf16[2,128,2048]{2,1,0:T(8,128)(2,1)} custom-call(s32[1,256]{1,0:T(1,128)S(1)} %bitcast.12, s32[3,16]{1,0:T(4,128)S(1)} %bitcast.20, bf16[2,128,2048]{2,1,0:T(8,128)(2,1)} %get-tuple-element.36.q_in, bf16[2,128,2048]{2,1,0:T(8,128)(2,1)} %get-tuple-element.37.k_in, bf16[2,128,2048]{2,1,0:T(8,128)(2,1)} %get-tuple-element.38.v_in), custom_call_target="tpu_custom_call" | custom-call | flops 2000000000 | bytes 4194304 | tf_op jit(solution)/shard_map/cond/branch_1_fun/pallas_call | solution.py:298
  101.0 2.3 %copy.11 = bf16[256,2048]{1,0:T(8,128)(2,1)} copy(bf16[256,2048]{1,0:T(8,128)(2,1)} %get-tuple-element.39) | data formatting | bytes 2097152
  (1 shorter events, 0.0 us)
Async XLA Ops:
  0.0 0.7 copy-start
  0.8 1.3 %copy-start.1 = (s32[16,3]{0,1:T(4,128)S(1)}, s32[16,3]{0,1:T(4,128)}, u32[]{:S(2)}) copy-start(s32[16,3]{0,1:T(4,128)} %param.10) | copy-start | bytes 580

commit v3 on v2

--- a/solution.py
+++ b/solution.py
@@ -30,18 +30,28 @@
 GOING = ((0, 0, 128), (1, 0, 64), (1, 64, 64))
 AHEAD = 3
 
-LEFT_OUT = ((2, 8, 10), ())
+FORMS = (
+    (2, 6, 8, 9, 10), (6, 7, 8, 13, 14), (2, 7, 8, 10, 14), (5, 6, 8, 10, 14),
+    (3, 6, 8, 9, 14), (3, 6, 8, 10, 13), (2, 6, 8, 10, 11), (6, 8, 14), (),
+)
 
 
 def spots(left_out):
     return tuple(offset for offset in range(1, SEQ) if offset not in left_out)
 
 
-def serves(plan, left_out):
+def first_form(plan):
     offset = (plan // BPG - jnp.arange(plan.shape[0], dtype=jnp.int32) // BPG) % SEQ
-    moved = (offset[None, :] - jnp.arange(SEQ, dtype=jnp.int32)[:, None]) % SEQ
-    misses = functools.reduce(jnp.logical_or, [moved == one for one in left_out])
-    return jnp.min(jnp.sum(misses.astype(jnp.int32), axis=1)) == 0
+    shift = jnp.arange(SEQ, dtype=jnp.int32)
+    moved = (offset[None, :] - shift[:, None]) % SEQ
+    against = jnp.zeros_like(moved)
+    for one in range(1, SEQ):
+        against = jnp.where(moved == one, sum(1 << n for n, left_out in enumerate(FORMS) if one in left_out), against)
+    against = lax.reduce(against, jnp.int32(0), lax.bitwise_or, (1,))
+    form = jnp.full((SEQ,), len(FORMS) - 1, jnp.int32)
+    for number in reversed(range(len(FORMS) - 1)):
+        form = jnp.where(against & (1 << number) == 0, number, form)
+    return jnp.min(form)
 
 
 def fill_tables(left_out, plan, here, columns):
@@ -101,8 +111,7 @@
 
     zbuf, xbuf, pbuf = (take(len(COMING)) for _ in range(3))
     opack, rbuf, zpack = (take(len(GOING)) for _ in range(3))
-    obuf = take(HEADS_HERE)
-    qg, kg, vg, columns, table, t_sem, z_send, z_recv, x_send, x_recv, y_send, y_recv, w_send, w_recv = scratch
+    obuf, qg, kg, vg, columns, table, t_sem, z_send, z_recv, x_send, x_recv, y_send, y_recv, w_send, w_recv = scratch
     inputs = (q_in, k_in, v_in)
     offsets = spots(left_out)
     s = lax.axis_index("seq")
@@ -110,6 +119,19 @@
 
     def across(offset):
         return (lax.rem(s + offset, SEQ), h)
+
+    def offset_of(spot):
+        offset = spot
+        for one in left_out:
+            offset = offset + (offset >= one).astype(jnp.int32)
+        return offset
+
+    def each(first, last, body):
+        def step(i, carry):
+            body(i)
+            return carry
+
+        lax.fori_loop(first, last, step, 0)
 
     def peer(step):
         return lax.rem(h + step, HEAD)
@@ -136,7 +158,8 @@
 
     def z_start(u):
         tensor, head, row, rows = COMING[u]
-        for step in range(1, HEAD):
+
+        def send(step):
             to = peer(step)
             pltpu.make_async_remote_copy(
                 src_ref=inputs[tensor].at[:, pl.ds(row, rows), columns_of(to, head)],
@@ -146,6 +169,8 @@
                 device_id=(s, to),
                 device_id_type=MESH,
             ).start()
+
+        each(1, HEAD, send)
         pltpu.make_async_copy(
             inputs[tensor].at[:, pl.ds(row, rows), columns_of(h, head)], zbuf[u].at[pl.ds(h * CAP, CAP)], z_recv.at[u]
         ).start()
@@ -154,28 +179,26 @@
         wait_for(zbuf[u], z_recv.at[u])
 
     def x_start(u):
-        for spot, offset in enumerate(offsets):
+        def send(spot):
             for j in range(CAP):
-                pbuf[u][spot * CAP + j] = zbuf[u][table[0, PACK + (spot + 1) * CAP + j]]
+                pbuf[u][(spot - 1) * CAP + j] = zbuf[u][table[0, PACK + spot * CAP + j]]
             pltpu.make_async_remote_copy(
-                src_ref=pbuf[u].at[pl.ds(spot * CAP, CAP)],
-                dst_ref=xbuf[u].at[pl.ds((spot + 1) * CAP, CAP)],
+                src_ref=pbuf[u].at[pl.ds((spot - 1) * CAP, CAP)],
+                dst_ref=xbuf[u].at[pl.ds(spot * CAP, CAP)],
                 send_sem=x_send.at[u],
                 recv_sem=x_recv.at[u],
-                device_id=across(offset),
+                device_id=across(offset_of(spot)),
                 device_id_type=MESH,
             ).start()
+
+        each(1, len(offsets) + 1, send)
         for j in range(CAP):
             xbuf[u][j] = zbuf[u][table[0, PACK + j]]
 
     def x_wait(u):
         wait_for(xbuf[u].at[pl.ds(CAP, len(offsets) * CAP)], x_recv.at[u])
 
-    def attend(head):
-        group = lax.rem(s + table[0, SHIFT], SEQ)
-        first_end = lengths[0, group]
-        second_end = first_end + lengths[1, group]
-
+    def collect(head):
         def gather(r, carry):
             index = table[0, PLACE + r]
             for u, (tensor, own, row, rows) in enumerate(COMING):
@@ -190,6 +213,11 @@
             return carry
 
         lax.fori_loop(0, BPG, gather, 0)
+
+    def attend(head):
+        group = lax.rem(s + table[0, SHIFT], SEQ)
+        first_end = lengths[0, group]
+        second_end = first_end + lengths[1, group]
         behind = lax.broadcasted_iota(jnp.int32, (1, WINDOW), 1) // BLOCK - PAD
         down = lax.broadcasted_iota(jnp.int32, (BLOCK, BLOCK), 0)
         along = lax.broadcasted_iota(jnp.int32, (BLOCK, BLOCK), 1)
@@ -213,38 +241,42 @@
             peak = jnp.max(scores, axis=1, keepdims=True)
             weights = jnp.exp2((scores - peak) * (SCALE * LOG2E)).astype(jnp.bfloat16)
             both = jnp.dot(weights, vg[window], preferred_element_type=jnp.float32)
-            obuf[head][i] = (both[:, :HEAD_DIM] / both[:, HEAD_DIM:]).astype(jnp.bfloat16)
+            obuf[head * BPG + i] = (both[:, :HEAD_DIM] / both[:, HEAD_DIM:]).astype(jnp.bfloat16)
             return carry
 
         lax.fori_loop(0, BPG, block, 0, unroll=4)
 
     def y_start(w):
         head, row, rows = GOING[w]
-        for spot, offset in enumerate(offsets):
+
+        def send(spot):
             for j in range(CAP):
-                opack[w][spot * CAP + j] = obuf[head][table[0, REPACK + (spot + 1) * CAP + j], row : row + rows]
+                opack[w][(spot - 1) * CAP + j] = obuf[table[0, REPACK + spot * CAP + j] + head * BPG, row : row + rows]
             pltpu.make_async_remote_copy(
-                src_ref=opack[w].at[pl.ds(spot * CAP, CAP)],
-                dst_ref=rbuf[w].at[pl.ds((spot + 1) * CAP, CAP)],
+                src_ref=opack[w].at[pl.ds((spot - 1) * CAP, CAP)],
+                dst_ref=rbuf[w].at[pl.ds(spot * CAP, CAP)],
                 send_sem=y_send.at[w],
                 recv_sem=y_recv.at[w],
-                device_id=across(SEQ - offset),
+                device_id=across(SEQ - offset_of(spot)),
                 device_id_type=MESH,
             ).start()
+
+        each(1, len(offsets) + 1, send)
         for j in range(CAP):
-            rbuf[w][j] = obuf[head][table[0, REPACK + j], row : row + rows]
+            rbuf[w][j] = obuf[table[0, REPACK + j] + head * BPG, row : row + rows]
 
     def w_start(w):
         head, row, rows = GOING[w]
         wait_for(rbuf[w].at[pl.ds(CAP, len(offsets) * CAP)], y_recv.at[w])
-        for step in range(1, HEAD + 1):
-            to = peer(step)
+        target = out.at[:, pl.ds(row, rows), columns_of(h, head)]
+
+        def pack(to):
             for j in range(CAP):
                 zpack[w][to, j] = rbuf[w][table[0, RETURN + to * CAP + j]]
-            target = out.at[:, pl.ds(row, rows), columns_of(h, head)]
-            if step == HEAD:
-                pltpu.make_async_copy(zpack[w].at[to], target, w_recv.at[w]).start()
-                continue
+
+        def send(step):
+            to = peer(step)
+            pack(to)
             pltpu.make_async_remote_copy(
                 src_ref=zpack[w].at[to],
                 dst_ref=target,
@@ -253,6 +285,10 @@
                 device_id=(s, to),
                 device_id_type=MESH,
             ).start()
+
+        each(1, HEAD, send)
+        pack(h)
+        pltpu.make_async_copy(zpack[w].at[h], target, w_recv.at[w]).start()
 
     for u in range(AHEAD):
         z_start(u)
@@ -264,14 +300,25 @@
             z_start(u + AHEAD)
     first = [u for u, unit in enumerate(COMING) if unit[1] == 0]
     second = [u for u, unit in enumerate(COMING) if unit[1] == 1]
-    for u in first:
-        x_wait(u)
-    attend(0)
-    for u in second[:-1]:
-        x_wait(u)
-    y_start(0)
-    x_wait(second[-1])
-    attend(1)
+
+    def one_head(head):
+        @pl.when(head == 0)
+        def _():
+            for u in first:
+                x_wait(u)
+            collect(0)
+
+        @pl.when(head == 1)
+        def _():
+            for u in second[:-1]:
+                x_wait(u)
+            y_start(0)
+            x_wait(second[-1])
+            collect(1)
+
+        attend(head)
+
+    each(0, HEADS_HERE, one_head)
     for w in range(1, len(GOING)):
         y_start(w)
     for w in range(len(GOING)):
@@ -307,8 +354,8 @@
         + [blocks(count * CAP, unit[2]) for unit in GOING]
         + [blocks((count + 1) * CAP, unit[2]) for unit in GOING]
         + [pltpu.VMEM((HEAD, CAP, unit[2], HEAD_DIM), bf16) for unit in GOING]
-        + [blocks(BPG, BLOCK)] * HEADS_HERE
         + [
+            blocks(HEADS_HERE * BPG, BLOCK),
             pltpu.VMEM((BPG * BLOCK, HEAD_DIM), bf16),
             pltpu.VMEM(((PAD + BPG) * BLOCK, HEAD_DIM), bf16),
             pltpu.VMEM(((PAD + BPG) * BLOCK, 2 * HEAD_DIM), bf16),
@@ -319,7 +366,7 @@
         + [in_flight(COMING)] * 4
         + [in_flight(GOING)] * 4,
         compiler_params=pltpu.CompilerParams(
-            collective_id=number, has_side_effects=True, vmem_limit_bytes=63 * 2**20
+            collective_id=number, has_side_effects=True, vmem_limit_bytes=50 * 2**20
         ),
         cost_estimate=pl.CostEstimate(flops=2_000_000_000, bytes_accessed=4 * 2**20, transcendentals=4_000_000),
     )(plan.reshape(1, -1), lengths.T, queries, keys, values)
@@ -327,8 +374,8 @@
 
 def local(queries, keys, values, lengths, plan):
     queries, keys, values = (array.reshape(CAP, BLOCK, -1) for array in (queries, keys, values))
-    forms = [functools.partial(exchange, number, left_out) for number, left_out in enumerate(LEFT_OUT)]
-    attended = lax.cond(serves(plan, LEFT_OUT[0]), *forms, queries, keys, values, lengths, plan)
+    forms = [functools.partial(exchange, number, left_out) for number, left_out in enumerate(FORMS)]
+    attended = lax.switch(first_form(plan), forms, queries, keys, values, lengths, plan)
     return attended.reshape(CAP * BLOCK, -1)
 
 

time: 103 us -> 89.2 us (0.87)
  Pallas kernels: 98.8 us -> 85.4 us
  local copies, waits for them, and re-layouts: 2.99 us -> 1.66 us
    pallas_call x1, Pallas kernels: 98.8 us -> 85.4 us  [exchange(): pl.pallas_call(functools.partial(kernel, left_out), out_shape=jax.ShapeDt...]
    unnamed x5, local copies, waits for them, and re-layouts: 2.99 us -> 1.66 us
where the time goes in v3:
time: 89.2 us; the launch traced here: 88.9 us
  Pallas kernels  85.4 us (96%)
  local copies, waits for them, and re-layouts  1.66 us (2%)
    pallas_call x1, Pallas kernels, exchange(): pl.pallas_call(functools.partial(kernel, left_out), out_shape=jax.ShapeDt...  85.4 us

profile of v3, /device:TPU:1, one launch (start us, length us, event | category | flops | bytes accessed | tf_op | source)
XLA Modules:
  0.0 88.9 jit_solution(6956148719028222972)
XLA Ops:
  0.0 0.0 copy-start
  0.0 0.7 copy-done
  0.7 0.0 copy-start.1
  0.7 0.1 select_reduce_fusion
  0.8 0.6 fusion.6
  1.5 0.0 copy-done.1
  2.1 85.7 %conditional.1 = (bf16[256,2048]{1,0:T(8,128)(2,1)S(1)}) conditional(s32[]{:T(128)} %clamp.3, (s32[256]{0:T(256)S(1)}, s32[16,3]{0,1:T(4,128)S(1)}, bf16[2,128,2048]{2,1,0:T(8,128)(2,1)}, bf16[2,128,2048]{2,1,0:T(8,128)(2,1)}, bf16[2,128,2048]{2,1,0:T(8,128)(2,1)}) %tuple.96, (s32[256]{0:T(256)S(1)}, ...), branch_computations={%region_2.3_spmd, %region_3.4_spmd, %region_4.5_spmd, %region_5.6_... | conditional | flops 2000000000 | bytes 4194312 | solution.py:378
  2.2 85.4 %branch_1_fun.1 = bf16[2,128,2048]{2,1,0:T(8,128)(2,1)S(1)} custom-call(s32[1,256]{1,0:T(1,128)S(1)} %bitcast.40, s32[3,16]{1,0:T(4,128)S(1)} %bitcast.76, bf16[2,128,2048]{2,1,0:T(8,128)(2,1)} %get-tuple-element.113.q_in, bf16[2,128,2048]{2,1,0:T(8,128)(2,1)} %get-tuple-element.114.k_in, bf16[2,128,2048]{2,1,0:T(8,128)(2,1)} %get-tuple-element.115.v_in), custom_call_target="tpu_custom_call" | custom-call | flops 2000000000 | bytes 4194304 | tf_op jit(solution)/shard_map/cond/branch_1_fun/pallas_call | solution.py:345
  87.9 1.0 %copy.25 = bf16[256,2048]{1,0:T(8,128)(2,1)} copy(bf16[256,2048]{1,0:T(8,128)(2,1)S(1)} %get-tuple-element.151) | data formatting | bytes 2097152
  (1 shorter events, 0.0 us)
Async XLA Ops:
  0.0 0.7 copy-start
  0.7 0.8 copy-start.1

commit v4 on v3

--- a/solution.py
+++ b/solution.py
@@ -11,6 +11,7 @@
 HEAD_DIM = 128
 BLOCK = 128
 SEQ = 16
+SIDE = 4
 HEAD = 8
 BPG = 16
 CAP = 2
@@ -24,11 +25,19 @@
 QUERY, KEY, VALUE = 0, 1, 2
 
 COMING = (
-    (KEY, 0, 0, 64), (KEY, 0, 64, 64), (QUERY, 0, 0, 128), (VALUE, 0, 0, 128),
-    (KEY, 1, 0, 128), (QUERY, 1, 0, 128), (VALUE, 1, 0, 128),
+    (KEY, 0, 0, 64),
+    (KEY, 0, 64, 64),
+    (QUERY, 0, 0, 64),
+    (QUERY, 0, 64, 64),
+    (VALUE, 0, 0, 64),
+    (VALUE, 0, 64, 64),
+    (KEY, 1, 0, 128),
+    (QUERY, 1, 0, 128),
+    (VALUE, 1, 0, 64),
+    (VALUE, 1, 64, 64),
 )
 GOING = ((0, 0, 128), (1, 0, 64), (1, 64, 64))
-AHEAD = 3
+AHEAD = 5
 
 FORMS = (
     (2, 6, 8, 9, 10), (6, 7, 8, 13, 14), (2, 7, 8, 10, 14), (5, 6, 8, 10, 14),
@@ -111,7 +120,7 @@
 
     zbuf, xbuf, pbuf = (take(len(COMING)) for _ in range(3))
     opack, rbuf, zpack = (take(len(GOING)) for _ in range(3))
-    obuf, qg, kg, vg, columns, table, t_sem, z_send, z_recv, x_send, x_recv, y_send, y_recv, w_send, w_recv = scratch
+    obuf, qg, kg, vg, columns, table, t_sem, all_in, z_send, z_recv, x_send, x_recv, y_send, y_recv, w_send, w_recv = scratch
     inputs = (q_in, k_in, v_in)
     offsets = spots(left_out)
     s = lax.axis_index("seq")
@@ -137,18 +146,16 @@
         return lax.rem(h + step, HEAD)
 
     barrier = pltpu.get_barrier_semaphore()
-    partners = sorted({offset for one in offsets for offset in (one, SEQ - one)})
     for step in range(1, HEAD):
         pl.semaphore_signal(barrier, inc=1, device_id=(s, peer(step)), device_id_type=MESH)
-    for offset in partners:
-        pl.semaphore_signal(barrier, inc=1, device_id=across(offset), device_id_type=MESH)
-    fill_tables(left_out, plan, s, columns)
-    fetch = pltpu.make_async_copy(columns, table, t_sem)
-    fetch.start()
-    kg[: PAD * BLOCK] = jnp.zeros((PAD * BLOCK, HEAD_DIM), jnp.bfloat16)
-    vg[: PAD * BLOCK, :HEAD_DIM] = jnp.zeros((PAD * BLOCK, HEAD_DIM), jnp.bfloat16)
-    vg[:, HEAD_DIM:] = jnp.ones(((PAD + BPG) * BLOCK, HEAD_DIM), jnp.bfloat16)
-    pl.semaphore_wait(barrier, len(partners) + HEAD - 1)
+    row, line = s // SIDE, s % SIDE
+    beside = [(row * SIDE + lax.rem(line + step, SIDE), h) for step in range(1, SIDE)]
+    above = [(lax.rem(row + step, SIDE) * SIDE + line, h) for step in range(1, SIDE)]
+    for device in above + beside:
+        pl.semaphore_signal(barrier, inc=1, device_id=device, device_id_type=MESH)
+    pl.semaphore_wait(barrier, HEAD - 1 + 2 * (SIDE - 1))
+    for device in beside:
+        pl.semaphore_signal(all_in, inc=1, device_id=device, device_id_type=MESH)
 
     def columns_of(device, head):
         return pl.ds(pl.multiple_of((device * HEADS_HERE + head) * HEAD_DIM, HEAD_DIM), HEAD_DIM)
@@ -244,7 +251,7 @@
             obuf[head * BPG + i] = (both[:, :HEAD_DIM] / both[:, HEAD_DIM:]).astype(jnp.bfloat16)
             return carry
 
-        lax.fori_loop(0, BPG, block, 0, unroll=4)
+        lax.fori_loop(0, BPG, block, 0, unroll=8)
 
     def y_start(w):
         head, row, rows = GOING[w]
@@ -292,7 +299,14 @@
 
     for u in range(AHEAD):
         z_start(u)
+    fill_tables(left_out, plan, s, columns)
+    fetch = pltpu.make_async_copy(columns, table, t_sem)
+    fetch.start()
+    kg[: PAD * BLOCK] = jnp.zeros((PAD * BLOCK, HEAD_DIM), jnp.bfloat16)
+    vg[: PAD * BLOCK, :HEAD_DIM] = jnp.zeros((PAD * BLOCK, HEAD_DIM), jnp.bfloat16)
+    vg[:, HEAD_DIM:] = jnp.ones(((PAD + BPG) * BLOCK, HEAD_DIM), jnp.bfloat16)
     fetch.wait()
+    pl.semaphore_wait(all_in, SIDE - 1)
     for u in range(len(COMING)):
         z_wait(u)
         x_start(u)
@@ -362,6 +376,7 @@
             pltpu.VMEM((8, BLOCK), jnp.int32),
             pltpu.SMEM((8, BLOCK), jnp.int32),
             pltpu.SemaphoreType.DMA,
+            pltpu.SemaphoreType.REGULAR,
         ]
         + [in_flight(COMING)] * 4
         + [in_flight(GOING)] * 4,

time: 89.2 us -> 86.3 us (0.967)
  Pallas kernels: 85.4 us -> 82.5 us
    pallas_call x1, Pallas kernels: 85.4 us -> 82.5 us  [exchange(): pl.pallas_call(functools.partial(kernel, left_out), out_shape=jax.ShapeDt...]
where the time goes in v4:
time: 86.3 us; the launch traced here: 86.2 us
  Pallas kernels  82.5 us (96%)
  local copies, waits for them, and re-layouts  1.66 us (2%)
    pallas_call x1, Pallas kernels, exchange(): pl.pallas_call(functools.partial(kernel, left_out), out_shape=jax.ShapeDt...  82.5 us

profile of v4, /device:TPU:1, one launch (start us, length us, event | category | flops | bytes accessed | tf_op | source)
XLA Modules:
  0.0 86.2 jit_solution(10914523365009939194)
XLA Ops:
  0.0 0.0 copy-start
  0.0 0.7 copy-done
  0.7 0.0 copy-start.1
  0.7 0.1 select_reduce_fusion
  0.8 0.6 fusion.6
  1.5 0.0 copy-done.1
  2.1 83.1 %conditional.1 = (bf16[256,2048]{1,0:T(8,128)(2,1)S(1)}) conditional(s32[]{:T(128)} %clamp.3, (s32[256]{0:T(256)S(1)}, s32[16,3]{0,1:T(4,128)S(1)}, bf16[2,128,2048]{2,1,0:T(8,128)(2,1)}, bf16[2,128,2048]{2,1,0:T(8,128)(2,1)}, bf16[2,128,2048]{2,1,0:T(8,128)(2,1)}) %tuple.96, (s32[256]{0:T(256)S(1)}, ...), branch_computations={%region_2.3_spmd, %region_3.4_spmd, %region_4.5_spmd, %region_5.6_... | conditional | flops 2000000000 | bytes 4194312 | solution.py:393
  2.2 82.5 %branch_0_fun.1 = bf16[2,128,2048]{2,1,0:T(8,128)(2,1)S(1)} custom-call(s32[1,256]{1,0:T(1,128)S(1)} %bitcast.39, s32[3,16]{1,0:T(4,128)S(1)} %bitcast.75, bf16[2,128,2048]{2,1,0:T(8,128)(2,1)} %get-tuple-element.100.q_in, bf16[2,128,2048]{2,1,0:T(8,128)(2,1)} %get-tuple-element.101.k_in, bf16[2,128,2048]{2,1,0:T(8,128)(2,1)} %get-tuple-element.108.v_in), custom_call_target="tpu_custom_call" | custom-call | flops 2000000000 | bytes 4194304 | tf_op jit(solution)/shard_map/cond/branch_0_fun/pallas_call | solution.py:359
  85.2 1.0 %copy.25 = bf16[256,2048]{1,0:T(8,128)(2,1)} copy(bf16[256,2048]{1,0:T(8,128)(2,1)S(1)} %get-tuple-element.151) | data formatting | bytes 2097152
  (1 shorter events, 0.0 us)
Async XLA Ops:
  0.0 0.7 copy-start
  0.7 0.8 copy-start.1
